TPU v7x, 32 devices: a whole 2x2x4 slice. The times are simulated.
32 devices in a mesh: patch: 8 (over z, x), grp: 4 (over y, core).
Axes of the slice: x: 2, y: 2, z: 4, core: 2. Of those that a mesh axis runs over, the one named last changes fastest.
Arguments:
- incident: float32 [16, 65536], P(None, ('patch', 'grp')), may hold values from -6 to 6
- self_term: float32 [65536], P(('patch', 'grp')), may hold values from 1 to 3
- near_field: bfloat16 [65536, 2304], P(('patch', 'grp')), may hold values from -0.125 to 0.125
- history: bfloat16 [8, 16, 65536], P(None, None, 'patch'), may hold values from -6 to 6
- ret_values: bfloat16 [8192, 128, 128], P(('patch', 'grp')), may hold values from -0.125 to 0.125
- slot_row: int32 [8192], P(('patch', 'grp')), may hold values from 0 to 15
- slot_col: int32 [8192], P(('patch', 'grp')), may hold values from 0 to 191
- slot_delay: int32 [8192], P(('patch', 'grp')), may hold values from 0 to 7
- live_count: int32 [32], P(('patch', 'grp')), may hold values from 32 to 256, as said below
Outputs:
- current: float32 [16, 65536], P(None, ('patch', 'grp'))
- newest: bfloat16 [16, 65536], P(None, 'patch')
Inputs may be any that keep to these rules, and one draw needn't show every extreme that they name: The first live_count[d] slots of shard d are live, the rest ignored; some shard has all 256 slots live.
All inputs are finite; a program needn't handle non-finite values.
Results may differ from a plain program's by a relative error of at most 0.0055.
Values may be sent and summed in bfloat16 or wider, within the bound.
A program may use at most 128 MiB of HBM per device.

v0:
```python
import jax
import jax.numpy as jnp
from jax import lax
from jax.sharding import PartitionSpec as P

BLK = 128
DELAYS = 8
SWEEPS = 4
RB = 16
SLOTS = 256


def extended_2(block, sides, width):
    for axis, dim in sides:
        count = lax.axis_size(axis)
        forward = [(i, i + 1) for i in range(count - 1)]
        backward = [(target, source) for source, target in forward]
        low = lax.ppermute(
            lax.slice_in_dim(block, block.shape[dim] - width, None, axis=dim), axis, forward
        )
        high = lax.ppermute(lax.slice_in_dim(block, 0, width, axis=dim), axis, backward)
        block = jnp.concatenate([low, block, high], axis=dim)
    return block


def body(
    incident, self_term, near_field, history, ret_values, slot_row, slot_col, slot_delay, live_count
):
    waves = incident.shape[0]
    own_cols = incident.shape[1]
    group_idx = lax.axis_index("grp")
    window = extended_2(history, (("patch", 2),), history.shape[2])
    grouped = window.reshape(DELAYS, waves, window.shape[2] // BLK, BLK)
    limit = live_count[0]
    blocks = grouped[slot_delay, :, slot_col, :]
    prods = jnp.einsum("swj,sij->swi", blocks, ret_values, preferred_element_type=jnp.float32)
    alive = (jnp.arange(SLOTS, dtype=jnp.int32) < limit).astype(jnp.float32)
    onehot = (slot_row[None, :] == jnp.arange(RB, dtype=jnp.int32)[:, None]).astype(
        jnp.float32
    ) * alive[None, :]
    retarded = jnp.einsum("rs,swi->wri", onehot, prods, precision=lax.Precision.HIGHEST)
    rhs = incident - retarded.reshape(waves, own_cols)
    sweep_in = lax.dynamic_slice_in_dim(history[0], group_idx * own_cols, own_cols, 1)
    current = sweep_in.astype(jnp.float32)
    for sweep in range(SWEEPS):
        extended = extended_2(sweep_in, (("patch", 1),), BLK)
        coupling = lax.dot_general(
            extended, near_field, (((1,), (1,)), ((), ())), preferred_element_type=jnp.float32
        )
        current = (rhs - coupling) / self_term[None, :]
        sweep_in = current.astype(jnp.bfloat16)
    newest = lax.all_gather(sweep_in, "grp", axis=1, tiled=True)
    return (current, newest)


def solution(mesh):
    placed = (
        P(None, ("patch", "grp")),
        P(("patch", "grp")),
        P(("patch", "grp"), None),
        P(None, None, "patch"),
        P(("patch", "grp"), None, None),
        P(("patch", "grp")),
        P(("patch", "grp")),
        P(("patch", "grp")),
        P(("patch", "grp")),
    )
    return jax.shard_map(
        body,
        mesh=mesh,
        in_specs=placed,
        out_specs=(P(None, ("patch", "grp")), P(None, "patch")),
        check_vma=False,
    )
```

profile of v0, /device:TPU:25, one launch (start us, length us, event | category | flops | bytes accessed | tf_op | source)
XLA Modules:
  0.0 165.2 jit_solution(814388530942626786)
XLA Ops:
  0.6 3.0 %collective-permute-start.1 = (bf16[8,16,8192]{2,1,0:T(8,128)(2,1)}, bf16[8,16,8192]{2,1,0:T(8,128)(2,1)S(1)}, u32[]{:S(2)}, u32[]{:S(2)}) collective-permute-start(bf16[8,16,8192]{2,1,0:T(8,128)(2,1)} %param.12), channel_id=1, source_target_pairs={{4,0},{8,4},{12,8},{16,12},{20,16},{24,20},{28,24},{5,1},{9,5},{13... | collective-permute-start | bytes 6291464 | tf_op jit(solution)/shard_map/ppermute | solution.py:21
  3.6 2.4 %collective-permute-start = (bf16[8,16,8192]{2,1,0:T(8,128)(2,1)}, bf16[8,16,8192]{2,1,0:T(8,128)(2,1)}, u32[]{:S(2)}, u32[]{:S(2)}) collective-permute-start(bf16[8,16,8192]{2,1,0:T(8,128)(2,1)} %param.12), channel_id=1, source_target_pairs={{0,4},{4,8},{8,12},{12,16},{16,20},{20,24},{24,28},{1,5},{5,9},{9,... | collective-permute-start | bytes 6291464 | tf_op jit(solution)/shard_map/ppermute | solution.py:18
  6.1 1.0 slice.27
  7.1 3.8 %collective-permute-start.3 = (bf16[16,128]{1,0:T(8,128)(2,1)S(1)}, bf16[16,128]{1,0:T(8,128)(2,1)S(1)}, u32[]{:S(2)}, u32[]{:S(2)}) collective-permute-start(bf16[16,128]{1,0:T(8,128)(2,1)S(1)} %get-tuple-element.9), channel_id=1, source_target_pairs={{4,0},{8,4},{12,8},{16,12},{20,16},{24,20},{28,24},{5,1},{9,5},{13... | collective-permute-start | bytes 12296 | tf_op jit(solution)/shard_map/ppermute | solution.py:21
  10.9 1.9 %collective-permute-start.2 = (bf16[16,128]{1,0:T(8,128)(2,1)S(1)}, bf16[16,128]{1,0:T(8,128)(2,1)S(1)}, u32[]{:S(2)}, u32[]{:S(2)}) collective-permute-start(bf16[16,128]{1,0:T(8,128)(2,1)S(1)} %get-tuple-element.8), channel_id=1, source_target_pairs={{0,4},{4,8},{8,12},{12,16},{16,20},{20,24},{24,28},{1,5},{5,9},{9,... | collective-permute-start | bytes 12296 | tf_op jit(solution)/shard_map/ppermute | solution.py:18
  13.4 0.7 fusion.36
  14.2 80.1 %collective-permute-done.1 = bf16[8,16,8192]{2,1,0:T(8,128)(2,1)S(1)} collective-permute-done((bf16[8,16,8192]{2,1,0:T(8,128)(2,1)}, bf16[8,16,8192]{2,1,0:T(8,128)(2,1)S(1)}, u32[]{:S(2)}, u32[]{:S(2)}) %collective-permute-start.1) | collective-permute-done | bytes 2097184 | tf_op jit(solution)/shard_map/ppermute | solution.py:21
  94.3 0.0 collective-permute-done
  94.3 7.2 %copy_bitcast_fusion = bf16[8,16,192,128]{3,1,2,0:T(8,128)(2,1)} fusion(bf16[8,16,8192]{2,1,0:T(8,128)(2,1)S(1)} %collective-permute-done.1, bf16[8,16,8192]{2,1,0:T(8,128)(2,1)} %param.12, bf16[8,16,8192]{2,1,0:T(8,128)(2,1)} %collective-permute-done), kind=kLoop, calls=%fused_computation.1 | loop fusion | flops 18874368 | bytes 12582912 | tf_op jit(solution)/shard_map/reshape | solution.py:33
  101.4 4.0 %gather_fusion = bf16[256,16,128]{2,1,0:T(8,128)(2,1)S(1)} fusion(bf16[8,16,192,128]{3,1,2,0:T(8,128)(2,1)} %copy_bitcast_fusion, s32[256]{0:T(256)S(1)} %fusion.36), kind=kCustom, calls=%fused_computation | custom fusion | bytes 2099200 | tf_op jit(solution)/shard_map/gather | solution.py:35
  105.4 0.0 copy-start.2
  105.5 0.0 copy-start.1
  105.5 0.0 copy-start
  105.5 0.0 slice-start
  105.5 0.0 slice-start.1
  105.5 6.9 %fusion.49 = f32[256,16,128]{2,1,0:T(8,128)S(1)} fusion(bf16[256,16,128]{2,1,0:T(8,128)(2,1)S(1)} %gather_fusion, bf16[256,128,128]{2,1,0:T(8,128)(2,1)} %param.13), kind=kOutput, calls=%fused_computation.62 | convolution fusion | flops 134217728 | bytes 11534336 | tf_op jit(solution)/shard_map/swj,sij->swi/dot_general | solution.py:36
  112.4 0.0 copy-done.2
  112.4 1.8 %fusion.7 = f32[16,128,16]{1,2,0:T(8,128)S(1)} fusion(f32[256,16,128]{2,1,0:T(8,128)S(1)} %fusion.49, f32[256]{0:T(256)S(1)} %compare_convert_fusion, s32[256]{0:T(256)S(1)} %copy-done.2), kind=kOutput, calls=%fused_computation.14 | convolution fusion | flops 100671488 | bytes 2230272 | tf_op jit(solution)/shard_map/rs,swi->wri/dot_general | solution.py:41
  114.2 0.0 copy-done.1
  114.2 0.1 bitcast_subtract_fusion
  114.2 0.0 slice-start.2
  114.3 0.0 collective-permute-done.3
  114.3 0.0 collective-permute-done.2
  114.3 0.0 copy-done
  114.3 6.3 %fusion.4 = bf16[16,2048]{1,0:T(8,128)(2,1)S(1)} fusion(f32[16,2048]{1,0:T(8,128)S(1)} %bitcast_subtract_fusion, bf16[2048,2304]{1,0:T(8,128)(2,1)} %param.11, bf16[16,128]{1,0:T(8,128)(2,1)S(1)} %collective-permute-done.3, bf16[16,2048]{1,0:T(8,128)(2,1)S(1)} %dynamic-slice_bitcast_fusion, bf16[16,128]{1,0:T(8,128)(2,1)S(1)} %collective-permute-done.2, ...), kind=kOutput, calls=%fused_computation.11 | convolution fusion | flops 151314432 | bytes 9715712 | tf_op jit(solution)/shard_map/dot_general | solution.py:47
  120.6 5.1 %collective-permute-start.5 = (bf16[16,128]{1,0:T(8,128)(2,1)S(1)}, bf16[16,128]{1,0:T(8,128)(2,1)S(1)}, u32[]{:S(2)}, u32[]{:S(2)}) collective-permute-start(bf16[16,128]{1,0:T(8,128)(2,1)S(1)} %get-tuple-element.7), channel_id=1, source_target_pairs={{4,0},{8,4},{12,8},{16,12},{20,16},{24,20},{28,24},{5,1},{9,5},{13... | collective-permute-start | bytes 12296 | tf_op jit(solution)/shard_map/ppermute | solution.py:21
  125.7 1.9 %collective-permute-start.4 = (bf16[16,128]{1,0:T(8,128)(2,1)S(1)}, bf16[16,128]{1,0:T(8,128)(2,1)S(1)}, u32[]{:S(2)}, u32[]{:S(2)}) collective-permute-start(bf16[16,128]{1,0:T(8,128)(2,1)S(1)} %get-tuple-element.6), channel_id=1, source_target_pairs={{0,4},{4,8},{8,12},{12,16},{16,20},{20,24},{24,28},{1,5},{5,9},{9,... | collective-permute-start | bytes 12296 | tf_op jit(solution)/shard_map/ppermute | solution.py:18
  127.6 0.0 collective-permute-done.5
  127.6 3.3 %collective-permute-done.4 = bf16[16,128]{1,0:T(8,128)(2,1)S(1)} collective-permute-done((bf16[16,128]{1,0:T(8,128)(2,1)S(1)}, bf16[16,128]{1,0:T(8,128)(2,1)S(1)}, u32[]{:S(2)}, u32[]{:S(2)}) %collective-permute-start.4) | collective-permute-done | bytes 4128 | tf_op jit(solution)/shard_map/ppermute | solution.py:18
  130.9 0.0 slice-done
  130.9 0.0 slice-done.1
  130.9 0.0 slice-done.2
  130.9 2.5 %fusion.5 = bf16[16,2048]{1,0:T(8,128)(2,1)S(1)} fusion(f32[16,2048]{1,0:T(8,128)S(1)} %bitcast_subtract_fusion, bf16[2048,2304]{1,0:T(8,128)(2,1)S(1)} %bitcast.23, bf16[16,128]{1,0:T(8,128)(2,1)S(1)} %collective-permute-done.5, bf16[16,2048]{1,0:T(8,128)(2,1)S(1)} %fusion.4, bf16[16,128]{1,0:T(8,128)(2,1)S(1)} %collective-permute-done.4, f32[2048]{0:T(1024)S(1)} %copy-done), kind=kOutput, calls=%fused_computation.12 | convolution fusion | flops 151314432 | bytes 9715712 | tf_op jit(solution)/shard_map/dot_general | solution.py:47
  133.5 1.9 %collective-permute-start.7 = (bf16[16,128]{1,0:T(8,128)(2,1)S(1)}, bf16[16,128]{1,0:T(8,128)(2,1)S(1)}, u32[]{:S(2)}, u32[]{:S(2)}) collective-permute-start(bf16[16,128]{1,0:T(8,128)(2,1)S(1)} %get-tuple-element.5), channel_id=1, source_target_pairs={{4,0},{8,4},{12,8},{16,12},{20,16},{24,20},{28,24},{5,1},{9,5},{13... | collective-permute-start | bytes 12296 | tf_op jit(solution)/shard_map/ppermute | solution.py:21
  135.4 3.4 %collective-permute-start.6 = (bf16[16,128]{1,0:T(8,128)(2,1)S(1)}, bf16[16,128]{1,0:T(8,128)(2,1)S(1)}, u32[]{:S(2)}, u32[]{:S(2)}) collective-permute-start(bf16[16,128]{1,0:T(8,128)(2,1)S(1)} %get-tuple-element.4), channel_id=1, source_target_pairs={{0,4},{4,8},{8,12},{12,16},{16,20},{20,24},{24,28},{1,5},{5,9},{9,... | collective-permute-start | bytes 12296 | tf_op jit(solution)/shard_map/ppermute | solution.py:18
  138.8 0.0 collective-permute-done.7
  138.8 1.9 %collective-permute-done.6 = bf16[16,128]{1,0:T(8,128)(2,1)S(1)} collective-permute-done((bf16[16,128]{1,0:T(8,128)(2,1)S(1)}, bf16[16,128]{1,0:T(8,128)(2,1)S(1)}, u32[]{:S(2)}, u32[]{:S(2)}) %collective-permute-start.6) | collective-permute-done | bytes 4128 | tf_op jit(solution)/shard_map/ppermute | solution.py:18
  140.7 2.5 %fusion.6 = bf16[16,2048]{1,0:T(8,128)(2,1)S(1)} fusion(f32[16,2048]{1,0:T(8,128)S(1)} %bitcast_subtract_fusion, bf16[2048,2304]{1,0:T(8,128)(2,1)S(1)} %bitcast.23, bf16[16,128]{1,0:T(8,128)(2,1)S(1)} %collective-permute-done.7, bf16[16,2048]{1,0:T(8,128)(2,1)S(1)} %fusion.5, bf16[16,128]{1,0:T(8,128)(2,1)S(1)} %collective-permute-done.6, f32[2048]{0:T(1024)S(1)} %copy-done), kind=kOutput, calls=%fused_computation.13 | convolution fusion | flops 151314432 | bytes 9715712 | tf_op jit(solution)/shard_map/dot_general | solution.py:47
  143.2 2.4 %collective-permute-start.9 = (bf16[16,128]{1,0:T(8,128)(2,1)S(1)}, bf16[16,128]{1,0:T(8,128)(2,1)S(1)}, u32[]{:S(2)}, u32[]{:S(2)}) collective-permute-start(bf16[16,128]{1,0:T(8,128)(2,1)S(1)} %get-tuple-element.3), channel_id=1, source_target_pairs={{4,0},{8,4},{12,8},{16,12},{20,16},{24,20},{28,24},{5,1},{9,5},{13... | collective-permute-start | bytes 12296 | tf_op jit(solution)/shard_map/ppermute | solution.py:21
  145.7 2.8 %collective-permute-start.8 = (bf16[16,128]{1,0:T(8,128)(2,1)S(1)}, bf16[16,128]{1,0:T(8,128)(2,1)S(1)}, u32[]{:S(2)}, u32[]{:S(2)}) collective-permute-start(bf16[16,128]{1,0:T(8,128)(2,1)S(1)} %get-tuple-element.2), channel_id=1, source_target_pairs={{0,4},{4,8},{8,12},{12,16},{16,20},{20,24},{24,28},{1,5},{5,9},{9,... | collective-permute-start | bytes 12296 | tf_op jit(solution)/shard_map/ppermute | solution.py:18
  148.5 0.0 collective-permute-done.9
  148.5 2.4 %collective-permute-done.8 = bf16[16,128]{1,0:T(8,128)(2,1)S(1)} collective-permute-done((bf16[16,128]{1,0:T(8,128)(2,1)S(1)}, bf16[16,128]{1,0:T(8,128)(2,1)S(1)}, u32[]{:S(2)}, u32[]{:S(2)}) %collective-permute-start.8) | collective-permute-done | bytes 4128 | tf_op jit(solution)/shard_map/ppermute | solution.py:18
  150.9 3.2 %fusion.48 = (bf16[16,2048]{1,0:T(8,128)(2,1)S(1)}, f32[16,2048]{1,0:T(8,128)}) fusion(f32[2048]{0:T(1024)S(1)} %copy-done, f32[16,2048]{1,0:T(8,128)S(1)} %bitcast_subtract_fusion, bf16[2048,2304]{1,0:T(8,128)(2,1)S(1)} %bitcast.23, bf16[16,128]{1,0:T(8,128)(2,1)S(1)} %collective-permute-done.9, bf16[16,2048]{1,0:T(8,128)(2,1)S(1)} %fusion.6, ...), kind=kOutput, calls=%fused_computation.61 | convolution fusion | flops 151314432 | bytes 9846784 | tf_op jit(solution)/shard_map/dot_general | solution.py:47
  154.1 10.3 %all_gather.3 = bf16[16,8192]{1,0:T(8,128)(2,1)S(1)} all-gather(bf16[16,2048]{1,0:T(8,128)(2,1)S(1)} %get-tuple-element.10), channel_id=1, replica_groups=mesh['patch'=8,'grp'=4] {'grp'}, dimensions={1}, use_global_device_ids=true | all-gather | bytes 327680 | tf_op jit(solution)/shard_map/all_gather | solution.py:52
  164.5 0.7 copy.21
  (7 shorter events, 0.1 us)
Async XLA Ops:
  0.6 93.6 %collective-permute-start.1 = (bf16[8,16,8192]{2,1,0:T(8,128)(2,1)}, bf16[8,16,8192]{2,1,0:T(8,128)(2,1)S(1)}, u32[]{:S(2)}, u32[]{:S(2)}) collective-permute-start(bf16[8,16,8192]{2,1,0:T(8,128)(2,1)} %param.12), channel_id=1, source_target_pairs={{4,0},{8,4},{12,8},{16,12},{20,16},{24,20},{28,24},{5,1},{9,5},{13... | collective-permute-start | bytes 6291464 | tf_op jit(solution)/shard_map/ppermute | solution.py:21
  3.6 90.6 %collective-permute-start = (bf16[8,16,8192]{2,1,0:T(8,128)(2,1)}, bf16[8,16,8192]{2,1,0:T(8,128)(2,1)}, u32[]{:S(2)}, u32[]{:S(2)}) collective-permute-start(bf16[8,16,8192]{2,1,0:T(8,128)(2,1)} %param.12), channel_id=1, source_target_pairs={{0,4},{4,8},{8,12},{12,16},{16,20},{20,24},{24,28},{1,5},{5,9},{9,... | collective-permute-start | bytes 6291464 | tf_op jit(solution)/shard_map/ppermute | solution.py:18
  7.1 107.2 %collective-permute-start.3 = (bf16[16,128]{1,0:T(8,128)(2,1)S(1)}, bf16[16,128]{1,0:T(8,128)(2,1)S(1)}, u32[]{:S(2)}, u32[]{:S(2)}) collective-permute-start(bf16[16,128]{1,0:T(8,128)(2,1)S(1)} %get-tuple-element.9), channel_id=1, source_target_pairs={{4,0},{8,4},{12,8},{16,12},{20,16},{24,20},{28,24},{5,1},{9,5},{13... | collective-permute-start | bytes 12296 | tf_op jit(solution)/shard_map/ppermute | solution.py:21
  10.9 103.4 %collective-permute-start.2 = (bf16[16,128]{1,0:T(8,128)(2,1)S(1)}, bf16[16,128]{1,0:T(8,128)(2,1)S(1)}, u32[]{:S(2)}, u32[]{:S(2)}) collective-permute-start(bf16[16,128]{1,0:T(8,128)(2,1)S(1)} %get-tuple-element.8), channel_id=1, source_target_pairs={{0,4},{4,8},{8,12},{12,16},{16,20},{20,24},{24,28},{1,5},{5,9},{9,... | collective-permute-start | bytes 12296 | tf_op jit(solution)/shard_map/ppermute | solution.py:18
  105.4 7.0 %copy-start.2 = (s32[256]{0:T(256)S(1)}, s32[256]{0:T(256)}, u32[]{:S(2)}) copy-start(s32[256]{0:T(256)} %param.14) | copy-start | bytes 3076
  105.5 8.7 %copy-start.1 = (f32[16,2048]{1,0:T(8,128)S(1)}, f32[16,2048]{1,0:T(8,128)}, u32[]{:S(2)}) copy-start(f32[16,2048]{1,0:T(8,128)} %param.9) | copy-start | bytes 393220
  105.5 8.8 %copy-start = (f32[2048]{0:T(1024)S(1)}, f32[2048]{0:T(1024)}, u32[]{:S(2)}) copy-start(f32[2048]{0:T(1024)} %param.10) | copy-start | bytes 24580
  105.5 25.4 %slice-start = ((s8[9437184]{0:T(1024)(128)(4,1)}), s8[4194304]{0:T(1024)(128)(4,1)S(1)}, s32[]{:S(2)}) async-start(s8[9437184]{0:T(1024)(128)(4,1)} %bitcast.22), calls=%async_computation | async-start | bytes 8388608
  105.5 25.4 %slice-start.1 = ((s8[9437184]{0:T(1024)(128)(4,1)}), s8[4194304]{0:T(1024)(128)(4,1)S(1)}, s32[]{:S(2)}) async-start(s8[9437184]{0:T(1024)(128)(4,1)} %bitcast.22), calls=%async_computation.1 | async-start | bytes 8388608
  114.2 16.7 %slice-start.2 = ((s8[9437184]{0:T(1024)(128)(4,1)}), s8[1048576]{0:T(1024)(128)(4,1)S(1)}, s32[]{:S(2)}) async-start(s8[9437184]{0:T(1024)(128)(4,1)} %bitcast.22), calls=%async_computation.2 | async-start | bytes 2097152
  120.6 7.0 %collective-permute-start.5 = (bf16[16,128]{1,0:T(8,128)(2,1)S(1)}, bf16[16,128]{1,0:T(8,128)(2,1)S(1)}, u32[]{:S(2)}, u32[]{:S(2)}) collective-permute-start(bf16[16,128]{1,0:T(8,128)(2,1)S(1)} %get-tuple-element.7), channel_id=1, source_target_pairs={{4,0},{8,4},{12,8},{16,12},{20,16},{24,20},{28,24},{5,1},{9,5},{13... | collective-permute-start | bytes 12296 | tf_op jit(solution)/shard_map/ppermute | solution.py:21
  125.7 5.3 %collective-permute-start.4 = (bf16[16,128]{1,0:T(8,128)(2,1)S(1)}, bf16[16,128]{1,0:T(8,128)(2,1)S(1)}, u32[]{:S(2)}, u32[]{:S(2)}) collective-permute-start(bf16[16,128]{1,0:T(8,128)(2,1)S(1)} %get-tuple-element.6), channel_id=1, source_target_pairs={{0,4},{4,8},{8,12},{12,16},{16,20},{20,24},{24,28},{1,5},{5,9},{9,... | collective-permute-start | bytes 12296 | tf_op jit(solution)/shard_map/ppermute | solution.py:18
  133.5 5.3 %collective-permute-start.7 = (bf16[16,128]{1,0:T(8,128)(2,1)S(1)}, bf16[16,128]{1,0:T(8,128)(2,1)S(1)}, u32[]{:S(2)}, u32[]{:S(2)}) collective-permute-start(bf16[16,128]{1,0:T(8,128)(2,1)S(1)} %get-tuple-element.5), channel_id=1, source_target_pairs={{4,0},{8,4},{12,8},{16,12},{20,16},{24,20},{28,24},{5,1},{9,5},{13... | collective-permute-start | bytes 12296 | tf_op jit(solution)/shard_map/ppermute | solution.py:21
  135.4 5.3 %collective-permute-start.6 = (bf16[16,128]{1,0:T(8,128)(2,1)S(1)}, bf16[16,128]{1,0:T(8,128)(2,1)S(1)}, u32[]{:S(2)}, u32[]{:S(2)}) collective-permute-start(bf16[16,128]{1,0:T(8,128)(2,1)S(1)} %get-tuple-element.4), channel_id=1, source_target_pairs={{0,4},{4,8},{8,12},{12,16},{16,20},{20,24},{24,28},{1,5},{5,9},{9,... | collective-permute-start | bytes 12296 | tf_op jit(solution)/shard_map/ppermute | solution.py:18
  143.2 5.3 %collective-permute-start.9 = (bf16[16,128]{1,0:T(8,128)(2,1)S(1)}, bf16[16,128]{1,0:T(8,128)(2,1)S(1)}, u32[]{:S(2)}, u32[]{:S(2)}) collective-permute-start(bf16[16,128]{1,0:T(8,128)(2,1)S(1)} %get-tuple-element.3), channel_id=1, source_target_pairs={{4,0},{8,4},{12,8},{16,12},{20,16},{24,20},{28,24},{5,1},{9,5},{13... | collective-permute-start | bytes 12296 | tf_op jit(solution)/shard_map/ppermute | solution.py:21
  145.7 5.3 %collective-permute-start.8 = (bf16[16,128]{1,0:T(8,128)(2,1)S(1)}, bf16[16,128]{1,0:T(8,128)(2,1)S(1)}, u32[]{:S(2)}, u32[]{:S(2)}) collective-permute-start(bf16[16,128]{1,0:T(8,128)(2,1)S(1)} %get-tuple-element.2), channel_id=1, source_target_pairs={{0,4},{4,8},{8,12},{12,16},{16,20},{20,24},{24,28},{1,5},{5,9},{9,... | collective-permute-start | bytes 12296 | tf_op jit(solution)/shard_map/ppermute | solution.py:18
where the time goes:
time: 166 us; the launch traced here: 165 us
  waiting for transfers between devices  87.7 us (53%)
  starting transfers between devices  28.6 us (17%)
  matrix products  23.2 us (14%)
  blocking collectives  10.3 us (6%)
  other arithmetic  7.93 us (5%)
  local copies, waits for them, and re-layouts  5.78 us (3%)
    ppermute x5, waiting for transfers between devices, extended_2(): lax.ppermute(lax.slice_in_dim(block, 0, width, axis=dim), axis, backward)  80.1 us
    ppermute x5, starting transfers between devices, extended_2(): lax.ppermute(lax.slice_in_dim(block, 0, width, axis=dim), axis, backward)  16.2 us
    dot_general x4, matrix products, body(): lax.dot_general(extended, near_field, (((1,), (1,)), ((), ())), preferred...  14.6 us
    ppermute x5, starting transfers between devices, extended_2(): lax.ppermute(lax.slice_in_dim(block, block.shape[dim] - width, None, axis...  12.5 us
    all_gather x1, blocking collectives, body(): newest = lax.all_gather(sweep_in, 'grp', axis=1, tiled=True)  10.3 us
    ppermute x5, waiting for transfers between devices, extended_2(): lax.ppermute(lax.slice_in_dim(block, block.shape[dim] - width, None, axis...  7.58 us
    reshape x1, other arithmetic, body(): grouped = window.reshape(DELAYS, waves, window.shape[2] // BLK, BLK)  7.17 us
    dot_general x1, matrix products, body(): jnp.einsum('swj,sij->swi', blocks, ret_values, preferred_element_type=jnp...  6.91 us
  transfers between devices with their start and end apart: 10, of which 4 were waited for; matrix products, arithmetic and copies ran while one was open for 13% of the time, Pallas kernels for 0%

commit v1 on v0

v1 whole, which is shorter than its diff:
```python
import functools

import jax
import jax.numpy as jnp
from jax import lax
from jax.experimental import pallas as pl
from jax.experimental.pallas import tpu as pltpu
from jax.sharding import PartitionSpec as P

BLK = 128
SWEEPS = 4
ONLY = 3
TILE = 512
UNROLL = 16
NT = (((1,), (1,)), ((), ()))


def kernel(
    n_patch,
    incident,
    self_term,
    near_hbm,
    hist_hbm,
    ret_hbm,
    row_vec,
    place,
    current,
    newest,
    win,
    blocks,
    near,
    ret,
    prods,
    reduced,
    rhs,
    acc,
    sweep_in,
    edges,
    local_sem,
    x_send,
    x_recv,
    z_send,
    z_recv,
    y_send,
    y_recv,
    c_send,
    c_recv,
    e_send,
    e_recv,
    n_send,
    n_recv,
):
    delays, waves, patch_cols = hist_hbm.shape
    own_cols = incident.shape[1]
    rb = own_cols // BLK
    slots = ret_hbm.shape[0]
    window_blocks = patch_cols // BLK
    half = patch_cols // 2
    fetched = delays - ONLY
    p = lax.axis_index("patch")
    g = lax.axis_index("grp")
    odd = lax.rem(p, 2)
    y = g // 2
    c = lax.rem(g, 2)
    g_core = y * 2 + (1 - c)
    g_plane = (1 - y) * 2 + c
    g_far = (1 - y) * 2 + (1 - c)
    x_peer = p + 1 - 2 * odd
    z_to = p + 2 - 4 * odd
    z_from = p - 2 + 4 * odd
    has_z_to = jnp.logical_and(z_to >= 0, z_to < n_patch)
    has_z_from = jnp.logical_and(z_from >= 0, z_from < n_patch)
    has_left = p > 0
    has_right = p < n_patch - 1
    x_side = 2 - 2 * odd
    z_side = 2 * odd

    def dev(patch, grp):
        return {"patch": patch, "grp": grp}

    def copy(src, dst, send, recv, device):
        return pltpu.make_async_remote_copy(
            src_ref=src,
            dst_ref=dst,
            send_sem=send,
            recv_sem=recv,
            device_id=device,
            device_id_type=pl.DeviceIdType.MESH,
        )

    load_hist = pltpu.make_async_copy(hist_hbm, win.at[1], local_sem.at[0])
    load_near = pltpu.make_async_copy(near_hbm, near, local_sem.at[1])
    load_ret = pltpu.make_async_copy(ret_hbm, ret, local_sem.at[2])
    load_hist.start()
    load_near.start()
    load_ret.start()

    barrier = pltpu.get_barrier_semaphore()

    def greet(patch, grp):
        pl.semaphore_signal(
            barrier, inc=1, device_id=dev(patch, grp), device_id_type=pl.DeviceIdType.MESH
        )

    for grp in (g_core, g_plane, g_far):
        greet(p, grp)
    pl.when(has_left)(lambda: greet(p - 1, g))
    pl.when(has_right)(lambda: greet(p + 1, g))
    pl.when(has_z_to)(lambda: greet(z_to, g))
    pl.when(has_z_from)(lambda: greet(z_from, g))
    met = 3
    for there in (has_left, has_right, has_z_to, has_z_from):
        met = met + there.astype(jnp.int32)
    pl.semaphore_wait(barrier, met)

    mine = pl.ds(pl.multiple_of(c * half, BLK), half)
    other = pl.ds(pl.multiple_of((1 - c) * half, BLK), half)

    def fetched_delay(j):
        return j + y * (delays - ONLY) if j < ONLY else j

    def plane_delay(j):
        return j + (1 - y) * (delays - ONLY)

    def unit(side, delay, cols):
        return win.at[side, delay, :, cols]

    def x_copy(j):
        d = fetched_delay(j)
        return copy(
            hist_hbm.at[d, :, mine], unit(z_side, d, mine), x_send.at[j], x_recv.at[j], dev(x_peer, g)
        )

    def x_arrival(j):
        d = fetched_delay(j)
        ref = unit(x_side, d, mine)
        return copy(ref, ref, x_send.at[j], x_recv.at[j], dev(x_peer, g))

    def z_copy(j):
        d = fetched_delay(j)
        return copy(
            unit(x_side, d, mine), unit(z_side, d, mine), z_send.at[j], z_recv.at[j], dev(z_to, g)
        )

    def z_arrival(j):
        ref = unit(z_side, fetched_delay(j), mine)
        return copy(ref, ref, z_send.at[j], z_recv.at[j], dev(z_from, g))

    def y_copy(kind, j):
        ref = unit((x_side, z_side)[kind], fetched_delay(j), mine)
        return copy(ref, ref, y_send.at[kind, j], y_recv.at[kind, j], dev(p, g_plane))

    def y_arrival(kind, j):
        ref = unit((x_side, z_side)[kind], plane_delay(j), mine)
        return copy(ref, ref, y_send.at[kind, j], y_recv.at[kind, j], dev(p, g_plane))

    def core_delay(i):
        return fetched_delay(i) if i < fetched else plane_delay(i - fetched)

    def core_copy(kind, i):
        ref = unit((x_side, z_side)[kind], core_delay(i), mine)
        return copy(ref, ref, c_send.at[kind, i], c_recv.at[kind, i], dev(p, g_core))

    def core_arrival(kind, i):
        ref = unit((x_side, z_side)[kind], core_delay(i), other)
        return copy(ref, ref, c_send.at[kind, i], c_recv.at[kind, i], dev(p, g_core))

    for j in range(fetched):
        x_copy(j).start()

    @pl.when(jnp.logical_not(has_z_from))
    def _():
        win[z_side] = jnp.zeros(win.shape[1:], win.dtype)
        count = delays * window_blocks
        blocks[pl.ds(z_side * count, count)] = jnp.zeros((count, waves, BLK), blocks.dtype)

    @pl.when(jnp.logical_not(has_left))
    def _():
        for k in range(SWEEPS - 1):
            edges[2 * k] = jnp.zeros((waves, BLK), edges.dtype)

    @pl.when(jnp.logical_not(has_right))
    def _():
        for k in range(SWEEPS - 1):
            edges[2 * k + 1] = jnp.zeros((waves, BLK), edges.dtype)

    def as_blocks(side, delay, part):
        first = part * (window_blocks // 2)
        base = (side * delays + delay) * window_blocks + first

        def some_blocks(step, _):
            for u in range(8):
                b = step * 8 + u
                cols = pl.ds(pl.multiple_of((first + b) * BLK, BLK), BLK)
                blocks[base + b] = win[side, delay, :, cols]
            return 0

        lax.fori_loop(0, window_blocks // 16, some_blocks, 0)

    def own_coupling(state, t):
        rows = pl.ds(pl.multiple_of(t * TILE, TILE), TILE)
        acc[:, rows] = lax.dot_general(
            state, near[rows, BLK : BLK + own_cols], NT, preferred_element_type=jnp.float32
        )

    own = pl.ds(pl.multiple_of(g * own_cols, BLK), own_cols)
    tiles = own_cols // TILE

    def first_coupling(t):
        if t == 0:
            load_hist.wait()
            load_near.wait()
        own_coupling(win[1, 0, :, own], t)

    def on_x(j):
        x_arrival(j).wait_recv()
        pl.when(has_z_to)(lambda: z_copy(j).start())
        if j < ONLY:
            y_copy(0, j).start()
        core_copy(0, j).start()
        as_blocks(x_side, fetched_delay(j), c)

    def on_z(j):
        @pl.when(has_z_from)
        def _():
            z_arrival(j).wait_recv()
            if j < ONLY:
                y_copy(1, j).start()
            core_copy(1, j).start()
            as_blocks(z_side, fetched_delay(j), c)

    def on_y(kind, j):
        def act():
            y_arrival(kind, j).wait_recv()
            core_copy(kind, fetched + j).start()
            as_blocks((x_side, z_side)[kind], plane_delay(j), c)

        act() if kind == 0 else pl.when(has_z_from)(act)

    for j in range(fetched + 4):
        if j < fetched:
            on_x(j)
        if 0 <= j - 1 < fetched:
            on_z(j - 1)
        if 0 <= j - 2 < ONLY:
            on_y(0, j - 2)
        if 0 <= j - 4 < ONLY:
            on_y(1, j - 4)
        if j < tiles:
            first_coupling(j)
        if j < delays:
            as_blocks(1, j, 0)
            as_blocks(1, j, 1)

    load_ret.wait()
    for i in range(delays):
        core_arrival(0, i).wait_recv()
        as_blocks(x_side, core_delay(i), 1 - c)

    @pl.when(has_z_from)
    def _():
        for i in range(delays):
            core_arrival(1, i).wait_recv()
            as_blocks(z_side, core_delay(i), 1 - c)

    def some_slots(step, _):
        for u in range(UNROLL):
            s = step * UNROLL + u
            held = blocks[place[s]]
            prods[pl.ds(pl.multiple_of(s * waves, waves), waves), :] = lax.dot_general(
                held, ret[s], NT, preferred_element_type=jnp.float32
            )
        return 0

    lax.fori_loop(0, slots // UNROLL, some_slots, 0)

    rows_of = lax.broadcasted_iota(jnp.int32, (rb, slots), 0)
    onehot = jnp.where(row_vec[...] == rows_of, 1.0, 0.0).astype(jnp.bfloat16)
    for w in range(waves):
        full = prods[pl.ds(w, slots, stride=waves), :]
        high = full.astype(jnp.bfloat16)
        low = (full - high.astype(jnp.float32)).astype(jnp.bfloat16)
        reduced[pl.ds(w * rb, rb), :] = jnp.dot(
            onehot, high, preferred_element_type=jnp.float32
        ) + jnp.dot(onehot, low, preferred_element_type=jnp.float32)
    for r in range(rb):
        cols = pl.ds(r * BLK, BLK)
        rhs[:, cols] = incident[:, cols] - reduced[pl.ds(r, waves, stride=rb), :]

    def edge_copy(k, to_right):
        if to_right:
            return copy(
                sweep_in.at[k, :, pl.ds(own_cols - BLK, BLK)],
                edges.at[2 * k],
                e_send.at[2 * k],
                e_recv.at[2 * k],
                dev(p + 1, g),
            )
        return copy(
            sweep_in.at[k, :, pl.ds(0, BLK)],
            edges.at[2 * k + 1],
            e_send.at[2 * k + 1],
            e_recv.at[2 * k + 1],
            dev(p - 1, g),
        )

    def edge_arrival(k, from_left):
        i = 2 * k if from_left else 2 * k + 1
        peer = p - 1 if from_left else p + 1
        return copy(edges.at[i], edges.at[i], e_send.at[i], e_recv.at[i], dev(peer, g))

    def newest_copy(i, t):
        part = pl.ds(t * TILE, TILE)
        there = pl.ds(pl.multiple_of(g * own_cols + t * TILE, BLK), TILE)
        return copy(
            sweep_in.at[SWEEPS - 1, :, part],
            newest.at[:, there],
            n_send.at[i, t],
            n_recv.at[i, t],
            dev(p, (g_core, g_plane, g_far)[i]),
        )

    def newest_arrival(i, t):
        source = (g_core, g_plane, g_far)[i]
        ref = newest.at[:, pl.ds(pl.multiple_of(source * own_cols + t * TILE, BLK), TILE)]
        return copy(ref, ref, n_send.at[i, t], n_recv.at[i, t], dev(p, source))

    order = [0, tiles - 1] + list(range(1, tiles - 1))
    for k in range(SWEEPS):
        last = k == SWEEPS - 1
        if k == 0:
            edge_block = pl.multiple_of(g * own_cols, BLK)
            left = win[0, 0, :, pl.ds(pl.multiple_of(edge_block + own_cols - BLK, BLK), BLK)]
            right = win[2, 0, :, pl.ds(edge_block, BLK)]
        else:
            state = sweep_in[k - 1]
            for t in range(tiles):
                own_coupling(state, t)
            pl.when(has_left)(lambda: edge_arrival(k - 1, True).wait_recv())
            pl.when(has_right)(lambda: edge_arrival(k - 1, False).wait_recv())
            left = edges[2 * (k - 1)]
            right = edges[2 * (k - 1) + 1]
        for t in order:
            cols = pl.ds(t * TILE, TILE)
            outer = lax.dot_general(
                left, near[cols, 0:BLK], NT, preferred_element_type=jnp.float32
            ) + lax.dot_general(
                right, near[cols, BLK + own_cols :], NT, preferred_element_type=jnp.float32
            )
            value = (rhs[:, cols] - (acc[:, cols] + outer)) / self_term[:, cols]
            rounded = value.astype(jnp.bfloat16)
            sweep_in[k, :, cols] = rounded
            if last:
                current[:, cols] = value
                for i in range(3):
                    newest_copy(i, t).start()
            elif t == 0:
                pl.when(has_left)(lambda: edge_copy(k, False).start())
            elif t == tiles - 1:
                pl.when(has_right)(lambda: edge_copy(k, True).start())

    newest[:, own] = sweep_in[SWEEPS - 1]

    for j in range(fetched):
        x_copy(j).wait_send()
        pl.when(has_z_to)(lambda: z_copy(j).wait_send())
    for i in range(delays):
        core_copy(0, i).wait_send()
    for j in range(ONLY):
        y_copy(0, j).wait_send()

    @pl.when(has_z_from)
    def _():
        for i in range(delays):
            core_copy(1, i).wait_send()
        for j in range(ONLY):
            y_copy(1, j).wait_send()

    for k in range(SWEEPS - 1):
        pl.when(has_left)(lambda: edge_copy(k, False).wait_send())
        pl.when(has_right)(lambda: edge_copy(k, True).wait_send())
    for t in range(tiles):
        for i in range(3):
            newest_copy(i, t).wait_send()
            newest_arrival(i, t).wait_recv()


def body(
    n_patch,
    incident,
    self_term,
    near_field,
    history,
    ret_values,
    slot_row,
    slot_col,
    slot_delay,
    live_count,
):
    delays, waves, patch_cols = history.shape
    own_cols = incident.shape[1]
    slots = ret_values.shape[0]
    rb = own_cols // BLK
    fetched = delays - ONLY
    tiles = own_cols // TILE
    window_blocks = patch_cols // BLK
    place = (
        slot_col // window_blocks * delays + slot_delay
    ) * window_blocks + slot_col % window_blocks
    live_row = jnp.where(jnp.arange(slots, dtype=jnp.int32) < live_count[0], slot_row, -1)
    dma = pltpu.SemaphoreType.DMA
    vmem = pl.BlockSpec(memory_space=pltpu.VMEM)
    smem = pl.BlockSpec(memory_space=pltpu.SMEM)
    anywhere = pl.BlockSpec(memory_space=pl.ANY)
    return pl.pallas_call(
        functools.partial(kernel, n_patch),
        out_shape=(
            jax.ShapeDtypeStruct((waves, own_cols), jnp.float32),
            jax.ShapeDtypeStruct((waves, patch_cols), jnp.bfloat16),
        ),
        in_specs=[vmem, vmem, anywhere, anywhere, anywhere, vmem, smem],
        out_specs=(vmem, vmem),
        scratch_shapes=[
            pltpu.VMEM((3, delays, waves, patch_cols), jnp.bfloat16),
            pltpu.VMEM((3 * delays * window_blocks, waves, BLK), jnp.bfloat16),
            pltpu.VMEM(near_field.shape, jnp.bfloat16),
            pltpu.VMEM(ret_values.shape, jnp.bfloat16),
            pltpu.VMEM((slots * waves, BLK), jnp.float32),
            pltpu.VMEM((waves * rb, BLK), jnp.float32),
            pltpu.VMEM((waves, own_cols), jnp.float32),
            pltpu.VMEM((waves, own_cols), jnp.float32),
            pltpu.VMEM((SWEEPS, waves, own_cols), jnp.bfloat16),
            pltpu.VMEM((2 * (SWEEPS - 1), waves, BLK), jnp.bfloat16),
            dma((3,)),
            dma((fetched,)),
            dma((fetched,)),
            dma((fetched,)),
            dma((fetched,)),
            dma((2, ONLY)),
            dma((2, ONLY)),
            dma((2, delays)),
            dma((2, delays)),
            dma((2 * (SWEEPS - 1),)),
            dma((2 * (SWEEPS - 1),)),
            dma((3, tiles)),
            dma((3, tiles)),
        ],
        compiler_params=pltpu.CompilerParams(
            collective_id=0, has_side_effects=True, vmem_limit_bytes=48 * 1024 * 1024
        ),
        cost_estimate=pl.CostEstimate(
            flops=2 * waves * own_cols * near_field.shape[1] * SWEEPS,
            bytes_accessed=2 * (near_field.size + ret_values.size + history.size),
            transcendentals=0,
        ),
    )(
        incident,
        self_term.reshape(1, own_cols),
        near_field,
        history,
        ret_values,
        live_row.reshape(1, slots),
        place,
    )


def solution(mesh):
    placed = (
        P(None, ("patch", "grp")),
        P(("patch", "grp")),
        P(("patch", "grp"), None),
        P(None, None, "patch"),
        P(("patch", "grp"), None, None),
        P(("patch", "grp")),
        P(("patch", "grp")),
        P(("patch", "grp")),
        P(("patch", "grp")),
    )
    return jax.shard_map(
        functools.partial(body, mesh.shape["patch"]),
        mesh=mesh,
        in_specs=placed,
        out_specs=(P(None, ("patch", "grp")), P(None, "patch")),
        check_vma=False,
    )
```

time: 166 us -> 58.2 us (0.35)
  the two profiles are of different devices: /device:TPU:25 before, /device:TPU:0 now
where the time goes in v1:
time: 58.2 us; the launch traced here: 57.9 us
  Pallas kernels  50.7 us (87%)
  local copies, waits for them, and re-layouts  4.55 us (8%)
  other arithmetic  1.39 us (2%)
  between operations  1.3 us (2%)
    pallas_call x1, Pallas kernels, body(): pl.pallas_call(functools.partial(kernel, n_patch), out_shape=(jax.ShapeDt...  50.7 us
    unnamed x8, local copies, waits for them, and re-layouts  4.55 us

profile of v1, /device:TPU:0, one launch (start us, length us, event | category | flops | bytes accessed | tf_op | source)
XLA Modules:
  0.0 57.9 jit_solution(13601688955686985825)
XLA Ops:
  1.3 0.7 %compare_select_fusion = s32[256]{0:T(256)S(1)} fusion(s32[256]{0:T(256)} %param.14, s32[]{:T(128)} %bitcast.3), kind=kLoop, calls=%fused_computation.2 | loop fusion | flops 512 | bytes 2052 | tf_op jit(solution)/shard_map/jit(_where)/select_n | solution.py:410
  2.0 0.7 %fusion.place = s32[256]{0:T(256)S(1)} fusion(s32[256]{0:T(256)} %param.16, s32[256]{0:T(256)} %param.15), kind=kLoop, calls=%fused_computation.6 | loop fusion | flops 5888 | bytes 3072 | tf_op jit(solution)/shard_map/add | solution.py:407
  2.7 0.0 copy-start
  2.7 1.6 %copy-done = bf16[8,16,8192]{2,1,0:T(8,128)(2,1)S(1)} copy-done((bf16[8,16,8192]{2,1,0:T(8,128)(2,1)S(1)}, bf16[8,16,8192]{2,1,0:T(8,128)(2,1)}, u32[]{:S(2)}) %copy-start) | copy-done | bytes 2097176
  4.3 0.0 copy-start.1
  4.3 0.9 %copy-done.1 = f32[16,2048]{1,0:T(8,128)S(1)} copy-done((f32[16,2048]{1,0:T(8,128)S(1)}, f32[16,2048]{1,0:T(8,128)}, u32[]{:S(2)}) %copy-start.1) | copy-done | bytes 131096
  5.2 0.0 copy-start.2
  5.2 0.7 %copy-done.2 = f32[2048]{0:T(1024)S(1)} copy-done((f32[2048]{0:T(1024)S(1)}, f32[2048]{0:T(1024)}, u32[]{:S(2)}) %copy-start.2) | copy-done | bytes 8216
  5.9 50.7 %shard_map.104 = (f32[16,2048]{1,0:T(8,128)S(1)}, bf16[16,8192]{1,0:T(8,128)(2,1)S(1)}) custom-call(f32[16,2048]{1,0:T(8,128)S(1)} %copy-done.1, f32[1,2048]{1,0:T(1,128)S(1)} %bitcast.4, bf16[2048,2304]{1,0:T(8,128)(2,1)} %near_hbm.1, bf16[8,16,8192]{2,1,0:T(8,128)(2,1)S(1)} %copy-done, bf16[256,128,128]{2,1,0:T(8,128)(2,1)} %ret_hbm.1, ...), custom_call_target="tpu_custom_call" | custom-call | flops 603979776 | bytes 19922944 | tf_op jit(solution)/shard_map/pallas_call | solution.py:415
  56.5 0.7 %copy.14 = f32[16,2048]{1,0:T(8,128)} copy(f32[16,2048]{1,0:T(8,128)S(1)} %get-tuple-element.4) | data formatting | bytes 262144
  57.2 0.7 %copy.15 = bf16[16,8192]{1,0:T(8,128)(2,1)} copy(bf16[16,8192]{1,0:T(8,128)(2,1)S(1)} %get-tuple-element.5) | data formatting | bytes 524288
Async XLA Ops:
  2.7 1.6 %copy-start = (bf16[8,16,8192]{2,1,0:T(8,128)(2,1)S(1)}, bf16[8,16,8192]{2,1,0:T(8,128)(2,1)}, u32[]{:S(2)}) copy-start(bf16[8,16,8192]{2,1,0:T(8,128)(2,1)} %hist_hbm.1) | copy-start | bytes 6291460
  4.3 0.9 %copy-start.1 = (f32[16,2048]{1,0:T(8,128)S(1)}, f32[16,2048]{1,0:T(8,128)}, u32[]{:S(2)}) copy-start(f32[16,2048]{1,0:T(8,128)} %incident.1) | copy-start | bytes 393220
  5.2 0.7 %copy-start.2 = (f32[2048]{0:T(1024)S(1)}, f32[2048]{0:T(1024)}, u32[]{:S(2)}) copy-start(f32[2048]{0:T(1024)} %param.10) | copy-start | bytes 24580

commit v2 on v1

--- a/solution.py
+++ b/solution.py
@@ -11,27 +11,35 @@
 SWEEPS = 4
 ONLY = 3
 TILE = 512
-UNROLL = 16
+UNROLL = 8
 NT = (((1,), (1,)), ((), ()))
 
 
 def kernel(
     n_patch,
-    incident,
-    self_term,
+    incident_hbm,
+    self_hbm,
     near_hbm,
     hist_hbm,
     ret_hbm,
-    row_vec,
-    place,
+    row_hbm,
+    col_hbm,
+    delay_hbm,
+    live_hbm,
     current,
     newest,
     win,
     blocks,
     near,
     ret,
-    prods,
-    reduced,
+    incident,
+    self_term,
+    slot_row,
+    slot_col,
+    slot_delay,
+    live,
+    picks,
+    retarded,
     rhs,
     acc,
     sweep_in,
@@ -51,7 +59,7 @@
     n_recv,
 ):
     delays, waves, patch_cols = hist_hbm.shape
-    own_cols = incident.shape[1]
+    own_cols = incident_hbm.shape[1]
     rb = own_cols // BLK
     slots = ret_hbm.shape[0]
     window_blocks = patch_cols // BLK
@@ -94,6 +102,21 @@
     load_hist.start()
     load_near.start()
     load_ret.start()
+    small = [
+        pltpu.make_async_copy(src, dst, local_sem.at[3 + i])
+        for i, (src, dst) in enumerate(
+            (
+                (incident_hbm, incident),
+                (self_hbm, self_term),
+                (row_hbm, slot_row),
+                (col_hbm, slot_col),
+                (delay_hbm, slot_delay),
+                (live_hbm, live),
+            )
+        )
+    ]
+    for one in small:
+        one.start()
 
     barrier = pltpu.get_barrier_semaphore()
 
@@ -168,11 +191,19 @@
     for j in range(fetched):
         x_copy(j).start()
 
+    picks[...] = jnp.zeros(picks.shape, picks.dtype)
+    for r in range(rb):
+        picks[r, r * waves : (r + 1) * waves, :] = jnp.ones((waves, BLK), picks.dtype)
+    retarded[...] = jnp.zeros(retarded.shape, retarded.dtype)
+
     @pl.when(jnp.logical_not(has_z_from))
     def _():
         win[z_side] = jnp.zeros(win.shape[1:], win.dtype)
-        count = delays * window_blocks
-        blocks[pl.ds(z_side * count, count)] = jnp.zeros((count, waves, BLK), blocks.dtype)
+        for d in range(delays):
+            start = (d * 3 + z_side) * window_blocks
+            blocks[pl.ds(start, window_blocks)] = jnp.zeros(
+                (window_blocks, waves, BLK), blocks.dtype
+            )
 
     @pl.when(jnp.logical_not(has_left))
     def _():
@@ -186,7 +217,7 @@
 
     def as_blocks(side, delay, part):
         first = part * (window_blocks // 2)
-        base = (side * delays + delay) * window_blocks + first
+        base = (delay * 3 + side) * window_blocks + first
 
         def some_blocks(step, _):
             for u in range(8):
@@ -253,6 +284,8 @@
             as_blocks(1, j, 1)
 
     load_ret.wait()
+    for one in small:
+        one.wait()
     for i in range(delays):
         core_arrival(0, i).wait_recv()
         as_blocks(x_side, core_delay(i), 1 - c)
@@ -263,29 +296,30 @@
             core_arrival(1, i).wait_recv()
             as_blocks(z_side, core_delay(i), 1 - c)
 
+    limit = live[0]
+
+    def picked(s):
+        row = jnp.where(s < limit, slot_row[s], rb)
+        held = blocks[slot_delay[s] * (3 * window_blocks) + slot_col[s]]
+        return picks[row] * jnp.tile(held, (rb, 1))
+
     def some_slots(step, _):
-        for u in range(UNROLL):
+        total = retarded[...]
+        for u in range(0, UNROLL, 2):
             s = step * UNROLL + u
-            held = blocks[place[s]]
-            prods[pl.ds(pl.multiple_of(s * waves, waves), waves), :] = lax.dot_general(
-                held, ret[s], NT, preferred_element_type=jnp.float32
+            total += lax.dot_general(
+                jnp.concatenate([picked(s), picked(s + 1)], axis=1),
+                jnp.concatenate([ret[s], ret[s + 1]], axis=1),
+                NT,
+                preferred_element_type=jnp.float32,
             )
+        retarded[...] = total
         return 0
 
     lax.fori_loop(0, slots // UNROLL, some_slots, 0)
-
-    rows_of = lax.broadcasted_iota(jnp.int32, (rb, slots), 0)
-    onehot = jnp.where(row_vec[...] == rows_of, 1.0, 0.0).astype(jnp.bfloat16)
-    for w in range(waves):
-        full = prods[pl.ds(w, slots, stride=waves), :]
-        high = full.astype(jnp.bfloat16)
-        low = (full - high.astype(jnp.float32)).astype(jnp.bfloat16)
-        reduced[pl.ds(w * rb, rb), :] = jnp.dot(
-            onehot, high, preferred_element_type=jnp.float32
-        ) + jnp.dot(onehot, low, preferred_element_type=jnp.float32)
     for r in range(rb):
         cols = pl.ds(r * BLK, BLK)
-        rhs[:, cols] = incident[:, cols] - reduced[pl.ds(r, waves, stride=rb), :]
+        rhs[:, cols] = incident[:, cols] - retarded[pl.ds(r * waves, waves), :]
 
     def edge_copy(k, to_right):
         if to_right:
@@ -404,34 +438,35 @@
     fetched = delays - ONLY
     tiles = own_cols // TILE
     window_blocks = patch_cols // BLK
-    place = (
-        slot_col // window_blocks * delays + slot_delay
-    ) * window_blocks + slot_col % window_blocks
-    live_row = jnp.where(jnp.arange(slots, dtype=jnp.int32) < live_count[0], slot_row, -1)
     dma = pltpu.SemaphoreType.DMA
     vmem = pl.BlockSpec(memory_space=pltpu.VMEM)
-    smem = pl.BlockSpec(memory_space=pltpu.SMEM)
-    anywhere = pl.BlockSpec(memory_space=pl.ANY)
+    in_hbm = pl.BlockSpec(memory_space=pltpu.HBM)
     return pl.pallas_call(
         functools.partial(kernel, n_patch),
         out_shape=(
             jax.ShapeDtypeStruct((waves, own_cols), jnp.float32),
             jax.ShapeDtypeStruct((waves, patch_cols), jnp.bfloat16),
         ),
-        in_specs=[vmem, vmem, anywhere, anywhere, anywhere, vmem, smem],
+        in_specs=[in_hbm] * 9,
         out_specs=(vmem, vmem),
         scratch_shapes=[
             pltpu.VMEM((3, delays, waves, patch_cols), jnp.bfloat16),
             pltpu.VMEM((3 * delays * window_blocks, waves, BLK), jnp.bfloat16),
             pltpu.VMEM(near_field.shape, jnp.bfloat16),
             pltpu.VMEM(ret_values.shape, jnp.bfloat16),
-            pltpu.VMEM((slots * waves, BLK), jnp.float32),
-            pltpu.VMEM((waves * rb, BLK), jnp.float32),
+            pltpu.VMEM((waves, own_cols), jnp.float32),
+            pltpu.VMEM((1, own_cols), jnp.float32),
+            pltpu.SMEM((slots,), jnp.int32),
+            pltpu.SMEM((slots,), jnp.int32),
+            pltpu.SMEM((slots,), jnp.int32),
+            pltpu.SMEM((1,), jnp.int32),
+            pltpu.VMEM((rb + 1, rb * waves, BLK), jnp.bfloat16),
+            pltpu.VMEM((rb * waves, BLK), jnp.float32),
             pltpu.VMEM((waves, own_cols), jnp.float32),
             pltpu.VMEM((waves, own_cols), jnp.float32),
             pltpu.VMEM((SWEEPS, waves, own_cols), jnp.bfloat16),
             pltpu.VMEM((2 * (SWEEPS - 1), waves, BLK), jnp.bfloat16),
-            dma((3,)),
+            dma((9,)),
             dma((fetched,)),
             dma((fetched,)),
             dma((fetched,)),
@@ -446,7 +481,7 @@
             dma((3, tiles)),
         ],
         compiler_params=pltpu.CompilerParams(
-            collective_id=0, has_side_effects=True, vmem_limit_bytes=48 * 1024 * 1024
+            collective_id=0, has_side_effects=True, vmem_limit_bytes=56 * 1024 * 1024
         ),
         cost_estimate=pl.CostEstimate(
             flops=2 * waves * own_cols * near_field.shape[1] * SWEEPS,
@@ -459,8 +494,10 @@
         near_field,
         history,
         ret_values,
-        live_row.reshape(1, slots),
-        place,
+        slot_row,
+        slot_col,
+        slot_delay,
+        live_count,
     )
 
 

time: 58.2 us -> 58.6 us (level)
  Pallas kernels: 50.7 us -> 53.9 us
  other arithmetic: 1.39 us -> 0 us
  local copies, waits for them, and re-layouts: 4.55 us -> 3.24 us
    pallas_call x1, Pallas kernels: 50.7 us -> 53.9 us  [body(): pl.pallas_call(functools.partial(kernel, n_patch), out_shape=(jax.ShapeDt...]
    unnamed x8 -> x2, local copies, waits for them, and re-layouts: 4.55 us -> 3.24 us
    add x1 -> x0, other arithmetic: 0.71 us -> none  [body(): (slot_col // window_blocks * delays + slot_delay) * window_blocks]
    select_n x1 -> x0, other arithmetic: 0.68 us -> none  [body(): jnp.where(jnp.arange(slots, dtype=jnp.int32) < live_count[0], slot_row, -1)]
where the time goes in v2:
time: 58.6 us; the launch traced here: 58.4 us
  Pallas kernels  53.9 us (92%)
  local copies, waits for them, and re-layouts  3.24 us (6%)
  between operations  1.29 us (2%)
    pallas_call x1, Pallas kernels, body(): pl.pallas_call(functools.partial(kernel, n_patch), out_shape=(jax.ShapeDt...  53.9 us
    unnamed x2, local copies, waits for them, and re-layouts  3.24 us

profile of v2, /device:TPU:0, one launch (start us, length us, event | category | flops | bytes accessed | tf_op | source)
XLA Modules:
  0.0 58.4 jit_solution(14921320454905969754)
XLA Ops:
  1.3 53.9 %shard_map.104 = (f32[16,2048]{1,0:T(8,128)}, bf16[16,8192]{1,0:T(8,128)(2,1)}) custom-call(f32[16,2048]{1,0:T(8,128)} %incident_hbm.1, f32[1,2048]{1,0:T(1,128)} %bitcast.1, bf16[2048,2304]{1,0:T(8,128)(2,1)} %near_hbm.1, bf16[8,16,8192]{2,1,0:T(8,128)(2,1)} %hist_hbm.1, bf16[256,128,128]{2,1,0:T(8,128)(2,1)} %ret_hbm.1, s32[256]{0:T(256)} %row_hbm.1, ...), custom_call_target="tpu_custom_call" | custom-call | flops 603979776 | bytes 19922944 | tf_op jit(solution)/shard_map/pallas_call | solution.py:444
  55.2 1.6 %copy.14 = f32[16,2048]{1,0:T(8,128)} copy(f32[16,2048]{1,0:T(8,128)} %get-tuple-element.4) | data formatting | bytes 262144
  56.7 1.7 %copy.15 = bf16[16,8192]{1,0:T(8,128)(2,1)} copy(bf16[16,8192]{1,0:T(8,128)(2,1)} %get-tuple-element.5) | data formatting | bytes 524288

commit v3 on v2

--- a/solution.py
+++ b/solution.py
@@ -12,6 +12,7 @@
 ONLY = 3
 TILE = 512
 UNROLL = 8
+GROUP = 4
 NT = (((1,), (1,)), ((), ()))
 
 
@@ -39,6 +40,7 @@
     slot_delay,
     live,
     picks,
+    prods,
     retarded,
     rhs,
     acc,
@@ -191,10 +193,12 @@
     for j in range(fetched):
         x_copy(j).start()
 
-    picks[...] = jnp.zeros(picks.shape, picks.dtype)
-    for r in range(rb):
-        picks[r, r * waves : (r + 1) * waves, :] = jnp.ones((waves, BLK), picks.dtype)
-    retarded[...] = jnp.zeros(retarded.shape, retarded.dtype)
+    wave_of = lax.broadcasted_iota(jnp.int32, (waves, rb * waves), 0)
+    lane_of = lax.broadcasted_iota(jnp.int32, (waves, rb * waves), 1)
+    for r in range(rb + 1):
+        picks[r] = jnp.where(lane_of == wave_of + r * waves, 1.0, 0.0).astype(
+            picks.dtype
+        ) if r < rb else jnp.zeros((waves, rb * waves), picks.dtype)
 
     @pl.when(jnp.logical_not(has_z_from))
     def _():
@@ -230,8 +234,8 @@
 
     def own_coupling(state, t):
         rows = pl.ds(pl.multiple_of(t * TILE, TILE), TILE)
-        acc[:, rows] = lax.dot_general(
-            state, near[rows, BLK : BLK + own_cols], NT, preferred_element_type=jnp.float32
+        acc[rows, :] = lax.dot_general(
+            near[rows, BLK : BLK + own_cols], state, NT, preferred_element_type=jnp.float32
         )
 
     own = pl.ds(pl.multiple_of(g * own_cols, BLK), own_cols)
@@ -297,26 +301,47 @@
             as_blocks(z_side, core_delay(i), 1 - c)
 
     limit = live[0]
-
-    def picked(s):
-        row = jnp.where(s < limit, slot_row[s], rb)
-        held = blocks[slot_delay[s] * (3 * window_blocks) + slot_col[s]]
-        return picks[row] * jnp.tile(held, (rb, 1))
+    none = jnp.zeros((waves, BLK), jnp.bfloat16)
 
     def some_slots(step, _):
-        total = retarded[...]
-        for u in range(0, UNROLL, 2):
+        strips = []
+        for first in range(0, UNROLL, GROUP):
+            held = []
+            for u in range(GROUP):
+                s = step * UNROLL + first + u
+                block = blocks[slot_delay[s] * (3 * window_blocks) + slot_col[s]]
+                held.append(
+                    jnp.concatenate([block if v == u else none for v in range(GROUP)], axis=1)
+                )
+            begin = step * UNROLL + first
+            strips.append(
+                lax.dot_general(
+                    jnp.concatenate([ret[begin + u] for u in range(GROUP)], axis=1),
+                    jnp.concatenate(held, axis=0),
+                    NT,
+                    preferred_element_type=jnp.float32,
+                )
+            )
+        full = jnp.concatenate(strips, axis=1)
+        high = full.astype(jnp.bfloat16)
+        low = (full - high.astype(jnp.float32)).astype(jnp.bfloat16)
+        prods[step, 0:BLK, :] = high
+        prods[step, BLK:, :] = low
+        return 0
+
+    lax.fori_loop(0, slots // UNROLL, some_slots, 0, unroll=2)
+    total = jnp.zeros((2 * BLK, rb * waves), jnp.float32)
+    for step in range(0, slots // UNROLL, 4):
+        chosen = []
+        for u in range(4 * UNROLL):
             s = step * UNROLL + u
-            total += lax.dot_general(
-                jnp.concatenate([picked(s), picked(s + 1)], axis=1),
-                jnp.concatenate([ret[s], ret[s + 1]], axis=1),
-                NT,
-                preferred_element_type=jnp.float32,
-            )
-        retarded[...] = total
-        return 0
-
-    lax.fori_loop(0, slots // UNROLL, some_slots, 0)
+            chosen.append(picks[jnp.where(s < limit, slot_row[s], rb)])
+        total += jnp.dot(
+            jnp.concatenate([prods[step + i] for i in range(4)], axis=1),
+            jnp.concatenate(chosen, axis=0),
+            preferred_element_type=jnp.float32,
+        )
+    retarded[...] = jnp.transpose(total[0:BLK] + total[BLK:])
     for r in range(rb):
         cols = pl.ds(r * BLK, BLK)
         rhs[:, cols] = incident[:, cols] - retarded[pl.ds(r * waves, waves), :]
@@ -374,14 +399,17 @@
             pl.when(has_right)(lambda: edge_arrival(k - 1, False).wait_recv())
             left = edges[2 * (k - 1)]
             right = edges[2 * (k - 1) + 1]
+        ends = jnp.concatenate([left, right], axis=1)
         for t in order:
             cols = pl.ds(t * TILE, TILE)
             outer = lax.dot_general(
-                left, near[cols, 0:BLK], NT, preferred_element_type=jnp.float32
-            ) + lax.dot_general(
-                right, near[cols, BLK + own_cols :], NT, preferred_element_type=jnp.float32
+                jnp.concatenate([near[cols, 0:BLK], near[cols, BLK + own_cols :]], axis=1),
+                ends,
+                NT,
+                preferred_element_type=jnp.float32,
             )
-            value = (rhs[:, cols] - (acc[:, cols] + outer)) / self_term[:, cols]
+            coupling = jnp.transpose(acc[cols, :] + outer)
+            value = (rhs[:, cols] - coupling) / self_term[:, cols]
             rounded = value.astype(jnp.bfloat16)
             sweep_in[k, :, cols] = rounded
             if last:
@@ -460,10 +488,11 @@
             pltpu.SMEM((slots,), jnp.int32),
             pltpu.SMEM((slots,), jnp.int32),
             pltpu.SMEM((1,), jnp.int32),
-            pltpu.VMEM((rb + 1, rb * waves, BLK), jnp.bfloat16),
+            pltpu.VMEM((rb + 1, waves, rb * waves), jnp.bfloat16),
+            pltpu.VMEM((slots // UNROLL, 2 * BLK, UNROLL * waves), jnp.bfloat16),
             pltpu.VMEM((rb * waves, BLK), jnp.float32),
             pltpu.VMEM((waves, own_cols), jnp.float32),
-            pltpu.VMEM((waves, own_cols), jnp.float32),
+            pltpu.VMEM((own_cols, waves), jnp.float32),
             pltpu.VMEM((SWEEPS, waves, own_cols), jnp.bfloat16),
             pltpu.VMEM((2 * (SWEEPS - 1), waves, BLK), jnp.bfloat16),
             dma((9,)),

time: 58.6 us -> 56.8 us (0.969)
  Pallas kernels: 53.9 us -> 52.1 us
    pallas_call x1, Pallas kernels: 53.9 us -> 52.1 us  [body(): pl.pallas_call(functools.partial(kernel, n_patch), out_shape=(jax.ShapeDt...]
where the time goes in v3:
time: 56.8 us; the launch traced here: 56.6 us
  Pallas kernels  52.1 us (92%)
  local copies, waits for them, and re-layouts  3.24 us (6%)
  between operations  1.29 us (2%)
    pallas_call x1, Pallas kernels, body(): pl.pallas_call(functools.partial(kernel, n_patch), out_shape=(jax.ShapeDt...  52.1 us
    unnamed x2, local copies, waits for them, and re-layouts  3.24 us

profile of v3, /device:TPU:0, one launch (start us, length us, event | category | flops | bytes accessed | tf_op | source)
XLA Modules:
  0.0 56.6 jit_solution(13600175469744880658)
XLA Ops:
  1.3 52.1 %shard_map.104 = (f32[16,2048]{1,0:T(8,128)}, bf16[16,8192]{1,0:T(8,128)(2,1)}) custom-call(f32[16,2048]{1,0:T(8,128)} %incident_hbm.1, f32[1,2048]{1,0:T(1,128)} %bitcast.1, bf16[2048,2304]{1,0:T(8,128)(2,1)} %near_hbm.1, bf16[8,16,8192]{2,1,0:T(8,128)(2,1)} %hist_hbm.1, bf16[256,128,128]{2,1,0:T(8,128)(2,1)} %ret_hbm.1, s32[256]{0:T(256)} %row_hbm.1, ...), custom_call_target="tpu_custom_call" | custom-call | flops 603979776 | bytes 19922944 | tf_op jit(solution)/shard_map/pallas_call | solution.py:472
  53.4 1.6 %copy.14 = f32[16,2048]{1,0:T(8,128)} copy(f32[16,2048]{1,0:T(8,128)} %get-tuple-element.4) | data formatting | bytes 262144
  54.9 1.7 %copy.15 = bf16[16,8192]{1,0:T(8,128)(2,1)} copy(bf16[16,8192]{1,0:T(8,128)(2,1)} %get-tuple-element.5) | data formatting | bytes 524288

commit v4 on v3

--- a/solution.py
+++ b/solution.py
@@ -9,7 +9,7 @@
 
 BLK = 128
 SWEEPS = 4
-ONLY = 3
+ONLY = 2
 TILE = 512
 UNROLL = 8
 GROUP = 4
@@ -27,7 +27,7 @@
     col_hbm,
     delay_hbm,
     live_hbm,
-    current,
+    current_hbm,
     newest,
     win,
     blocks,
@@ -43,6 +43,7 @@
     prods,
     retarded,
     rhs,
+    current,
     acc,
     sweep_in,
     edges,
@@ -59,6 +60,7 @@
     e_recv,
     n_send,
     n_recv,
+    out_sem,
 ):
     delays, waves, patch_cols = hist_hbm.shape
     own_cols = incident_hbm.shape[1]
@@ -368,21 +370,30 @@
         peer = p - 1 if from_left else p + 1
         return copy(edges.at[i], edges.at[i], e_send.at[i], e_recv.at[i], dev(peer, g))
 
+    peers = (g_core, g_plane, g_far)
+
     def newest_copy(i, t):
         part = pl.ds(t * TILE, TILE)
-        there = pl.ds(pl.multiple_of(g * own_cols + t * TILE, BLK), TILE)
         return copy(
             sweep_in.at[SWEEPS - 1, :, part],
-            newest.at[:, there],
+            newest.at[g, :, part],
             n_send.at[i, t],
             n_recv.at[i, t],
-            dev(p, (g_core, g_plane, g_far)[i]),
+            dev(p, peers[i]),
         )
 
     def newest_arrival(i, t):
-        source = (g_core, g_plane, g_far)[i]
-        ref = newest.at[:, pl.ds(pl.multiple_of(source * own_cols + t * TILE, BLK), TILE)]
-        return copy(ref, ref, n_send.at[i, t], n_recv.at[i, t], dev(p, source))
+        ref = newest.at[peers[i], :, pl.ds(t * TILE, TILE)]
+        return copy(ref, ref, n_send.at[i, t], n_recv.at[i, t], dev(p, peers[i]))
+
+    def out_copies(t):
+        part = pl.ds(t * TILE, TILE)
+        return (
+            pltpu.make_async_copy(current.at[:, part], current_hbm.at[:, part], out_sem.at[0, t]),
+            pltpu.make_async_copy(
+                sweep_in.at[SWEEPS - 1, :, part], newest.at[g, :, part], out_sem.at[1, t]
+            ),
+        )
 
     order = [0, tiles - 1] + list(range(1, tiles - 1))
     for k in range(SWEEPS):
@@ -409,19 +420,19 @@
                 preferred_element_type=jnp.float32,
             )
             coupling = jnp.transpose(acc[cols, :] + outer)
-            value = (rhs[:, cols] - coupling) / self_term[:, cols]
-            rounded = value.astype(jnp.bfloat16)
+            value = rhs[:, cols] - coupling
+            rounded = (value / self_term[:, cols]).astype(jnp.bfloat16)
             sweep_in[k, :, cols] = rounded
             if last:
                 current[:, cols] = value
                 for i in range(3):
                     newest_copy(i, t).start()
+                for one in out_copies(t):
+                    one.start()
             elif t == 0:
                 pl.when(has_left)(lambda: edge_copy(k, False).start())
             elif t == tiles - 1:
                 pl.when(has_right)(lambda: edge_copy(k, True).start())
-
-    newest[:, own] = sweep_in[SWEEPS - 1]
 
     for j in range(fetched):
         x_copy(j).wait_send()
@@ -442,6 +453,8 @@
         pl.when(has_left)(lambda: edge_copy(k, False).wait_send())
         pl.when(has_right)(lambda: edge_copy(k, True).wait_send())
     for t in range(tiles):
+        for one in out_copies(t):
+            one.wait()
         for i in range(3):
             newest_copy(i, t).wait_send()
             newest_arrival(i, t).wait_recv()
@@ -467,16 +480,15 @@
     tiles = own_cols // TILE
     window_blocks = patch_cols // BLK
     dma = pltpu.SemaphoreType.DMA
-    vmem = pl.BlockSpec(memory_space=pltpu.VMEM)
     in_hbm = pl.BlockSpec(memory_space=pltpu.HBM)
-    return pl.pallas_call(
+    numerator, newest = pl.pallas_call(
         functools.partial(kernel, n_patch),
         out_shape=(
             jax.ShapeDtypeStruct((waves, own_cols), jnp.float32),
-            jax.ShapeDtypeStruct((waves, patch_cols), jnp.bfloat16),
+            jax.ShapeDtypeStruct((patch_cols // own_cols, waves, own_cols), jnp.bfloat16),
         ),
         in_specs=[in_hbm] * 9,
-        out_specs=(vmem, vmem),
+        out_specs=(in_hbm, in_hbm),
         scratch_shapes=[
             pltpu.VMEM((3, delays, waves, patch_cols), jnp.bfloat16),
             pltpu.VMEM((3 * delays * window_blocks, waves, BLK), jnp.bfloat16),
@@ -491,6 +503,7 @@
             pltpu.VMEM((rb + 1, waves, rb * waves), jnp.bfloat16),
             pltpu.VMEM((slots // UNROLL, 2 * BLK, UNROLL * waves), jnp.bfloat16),
             pltpu.VMEM((rb * waves, BLK), jnp.float32),
+            pltpu.VMEM((waves, own_cols), jnp.float32),
             pltpu.VMEM((waves, own_cols), jnp.float32),
             pltpu.VMEM((own_cols, waves), jnp.float32),
             pltpu.VMEM((SWEEPS, waves, own_cols), jnp.bfloat16),
@@ -508,6 +521,7 @@
             dma((2 * (SWEEPS - 1),)),
             dma((3, tiles)),
             dma((3, tiles)),
+            dma((2, tiles)),
         ],
         compiler_params=pltpu.CompilerParams(
             collective_id=0, has_side_effects=True, vmem_limit_bytes=56 * 1024 * 1024
@@ -528,6 +542,7 @@
         slot_delay,
         live_count,
     )
+    return numerator / self_term[None, :], newest.transpose(1, 0, 2).reshape(waves, patch_cols)
 
 
 def solution(mesh):

time: 56.8 us -> 58.1 us (1.023)
  other arithmetic: 0 us -> 1.58 us
  local copies, waits for them, and re-layouts: 3.24 us -> 1.67 us
  Pallas kernels: 52.1 us -> 53.4 us
    unnamed x2, local copies, waits for them, and re-layouts: 3.24 us -> 0.01 us
    reshape x0 -> x1, local copies, waits for them, and re-layouts: none -> 1.67 us  [body(): newest.transpose(1, 0, 2).reshape(waves, patch_cols)]
    div x0 -> x1, other arithmetic: none -> 1.58 us  [body(): numerator / self_term[None, :]]
    pallas_call x1, Pallas kernels: 52.1 us -> 53.4 us  [body(): pl.pallas_call(functools.partial(kernel, n_patch), out_shape=(jax.ShapeDt...]
where the time goes in v4:
time: 58.1 us; the launch traced here: 57.9 us
  Pallas kernels  53.4 us (92%)
  local copies, waits for them, and re-layouts  1.67 us (3%)
  other arithmetic  1.58 us (3%)
  between operations  1.3 us (2%)
    pallas_call x1, Pallas kernels, body(): pl.pallas_call(functools.partial(kernel, n_patch), out_shape=(jax.ShapeDt...  53.4 us
    reshape x1, local copies, waits for them, and re-layouts, body(): newest.transpose(1, 0, 2).reshape(waves, patch_cols)  1.67 us
    div x1, other arithmetic, body(): numerator / self_term[None, :]  1.58 us

profile of v4, /device:TPU:0, one launch (start us, length us, event | category | flops | bytes accessed | tf_op | source)
XLA Modules:
  0.0 57.9 jit_solution(14467803750946600133)
XLA Ops:
  1.3 0.0 copy-start
  1.3 53.4 %shard_map.104 = (f32[16,2048]{1,0:T(8,128)}, bf16[4,16,2048]{2,1,0:T(8,128)(2,1)}) custom-call(f32[16,2048]{1,0:T(8,128)} %incident_hbm.1, f32[1,2048]{1,0:T(1,128)} %bitcast.6, bf16[2048,2304]{1,0:T(8,128)(2,1)} %near_hbm.1, bf16[8,16,8192]{2,1,0:T(8,128)(2,1)} %hist_hbm.1, bf16[256,128,128]{2,1,0:T(8,128)(2,1)} %ret_hbm.1, s32[256]{0:T(256)} %row_hbm.1, ...), custom_call_target="tpu_custom_call" | custom-call | flops 603979776 | bytes 19922944 | tf_op jit(solution)/shard_map/pallas_call | solution.py:484
  54.7 0.0 copy-done
  54.7 1.6 %broadcast_divide_fusion = f32[16,2048]{1,0:T(8,128)} fusion(f32[16,2048]{1,0:T(8,128)} %get-tuple-element.4, f32[2048]{0:T(1024)S(1)} %copy-done), kind=kLoop, calls=%fused_computation | loop fusion | flops 32768 | bytes 270336 | tf_op jit(solution)/shard_map/div | solution.py:545
  56.2 1.7 %copy.12 = bf16[4,2,8,2048]{3,2,0,1:T(8,128)(2,1)} copy(bf16[4,2,8,2048]{3,2,1,0:T(8,128)(2,1)} %bitcast.5) | data formatting | bytes 524288 | tf_op jit(solution)/shard_map/reshape | solution.py:545
Async XLA Ops:
  1.3 53.4 %copy-start = (f32[2048]{0:T(1024)S(1)}, f32[2048]{0:T(1024)}, u32[]{:S(2)}) copy-start(f32[2048]{0:T(1024)} %param.10) | copy-start | bytes 24580

commit v5 on v4

--- a/solution.py
+++ b/solution.py
@@ -9,7 +9,8 @@
 
 BLK = 128
 SWEEPS = 4
-ONLY = 2
+PARTS = 2
+ONLY = 5
 TILE = 512
 UNROLL = 8
 GROUP = 4
@@ -68,7 +69,9 @@
     slots = ret_hbm.shape[0]
     window_blocks = patch_cols // BLK
     half = patch_cols // 2
-    fetched = delays - ONLY
+    units = delays * PARTS
+    unit_cols = half // PARTS
+    fetched = units - ONLY
     p = lax.axis_index("patch")
     g = lax.axis_index("grp")
     odd = lax.rem(p, 2)
@@ -140,56 +143,53 @@
         met = met + there.astype(jnp.int32)
     pl.semaphore_wait(barrier, met)
 
-    mine = pl.ds(pl.multiple_of(c * half, BLK), half)
-    other = pl.ds(pl.multiple_of((1 - c) * half, BLK), half)
-
-    def fetched_delay(j):
-        return j + y * (delays - ONLY) if j < ONLY else j
-
-    def plane_delay(j):
-        return j + (1 - y) * (delays - ONLY)
-
-    def unit(side, delay, cols):
-        return win.at[side, delay, :, cols]
+    def fetched_unit(j):
+        return j + y * (units - ONLY) if j < ONLY else j
+
+    def plane_unit(j):
+        return j + (1 - y) * (units - ONLY)
+
+    def columns(core, i):
+        start = core * half + lax.rem(i, PARTS) * unit_cols
+        return pl.ds(pl.multiple_of(start, BLK), unit_cols)
+
+    def unit(side, i, core=c):
+        return win.at[side, i // PARTS, :, columns(core, i)]
 
     def x_copy(j):
-        d = fetched_delay(j)
-        return copy(
-            hist_hbm.at[d, :, mine], unit(z_side, d, mine), x_send.at[j], x_recv.at[j], dev(x_peer, g)
-        )
+        i = fetched_unit(j)
+        src = hist_hbm.at[i // PARTS, :, columns(c, i)]
+        return copy(src, unit(z_side, i), x_send.at[j], x_recv.at[j], dev(x_peer, g))
 
     def x_arrival(j):
-        d = fetched_delay(j)
-        ref = unit(x_side, d, mine)
+        ref = unit(x_side, fetched_unit(j))
         return copy(ref, ref, x_send.at[j], x_recv.at[j], dev(x_peer, g))
 
     def z_copy(j):
-        d = fetched_delay(j)
-        return copy(
-            unit(x_side, d, mine), unit(z_side, d, mine), z_send.at[j], z_recv.at[j], dev(z_to, g)
-        )
+        i = fetched_unit(j)
+        return copy(unit(x_side, i), unit(z_side, i), z_send.at[j], z_recv.at[j], dev(z_to, g))
 
     def z_arrival(j):
-        ref = unit(z_side, fetched_delay(j), mine)
+        ref = unit(z_side, fetched_unit(j))
         return copy(ref, ref, z_send.at[j], z_recv.at[j], dev(z_from, g))
 
     def y_copy(kind, j):
-        ref = unit((x_side, z_side)[kind], fetched_delay(j), mine)
+        ref = unit((x_side, z_side)[kind], fetched_unit(j))
         return copy(ref, ref, y_send.at[kind, j], y_recv.at[kind, j], dev(p, g_plane))
 
     def y_arrival(kind, j):
-        ref = unit((x_side, z_side)[kind], plane_delay(j), mine)
+        ref = unit((x_side, z_side)[kind], plane_unit(j))
         return copy(ref, ref, y_send.at[kind, j], y_recv.at[kind, j], dev(p, g_plane))
 
-    def core_delay(i):
-        return fetched_delay(i) if i < fetched else plane_delay(i - fetched)
+    def core_unit(i):
+        return fetched_unit(i) if i < fetched else plane_unit(i - fetched)
 
     def core_copy(kind, i):
-        ref = unit((x_side, z_side)[kind], core_delay(i), mine)
+        ref = unit((x_side, z_side)[kind], core_unit(i))
         return copy(ref, ref, c_send.at[kind, i], c_recv.at[kind, i], dev(p, g_core))
 
     def core_arrival(kind, i):
-        ref = unit((x_side, z_side)[kind], core_delay(i), other)
+        ref = unit((x_side, z_side)[kind], core_unit(i), 1 - c)
         return copy(ref, ref, c_send.at[kind, i], c_recv.at[kind, i], dev(p, g_core))
 
     for j in range(fetched):
@@ -221,8 +221,12 @@
         for k in range(SWEEPS - 1):
             edges[2 * k + 1] = jnp.zeros((waves, BLK), edges.dtype)
 
-    def as_blocks(side, delay, part):
-        first = part * (window_blocks // 2)
+    unit_blocks = unit_cols // BLK
+
+    def as_blocks(side, i, core):
+        i = jnp.int32(i)
+        first = (core * PARTS + lax.rem(i, PARTS)) * unit_blocks
+        delay = i // PARTS
         base = (delay * 3 + side) * window_blocks + first
 
         def some_blocks(step, _):
@@ -232,7 +236,7 @@
                 blocks[base + b] = win[side, delay, :, cols]
             return 0
 
-        lax.fori_loop(0, window_blocks // 16, some_blocks, 0)
+        lax.fori_loop(0, unit_blocks // 8, some_blocks, 0)
 
     def own_coupling(state, t):
         rows = pl.ds(pl.multiple_of(t * TILE, TILE), TILE)
@@ -255,7 +259,7 @@
         if j < ONLY:
             y_copy(0, j).start()
         core_copy(0, j).start()
-        as_blocks(x_side, fetched_delay(j), c)
+        as_blocks(x_side, fetched_unit(j), c)
 
     def on_z(j):
         @pl.when(has_z_from)
@@ -264,44 +268,49 @@
             if j < ONLY:
                 y_copy(1, j).start()
             core_copy(1, j).start()
-            as_blocks(z_side, fetched_delay(j), c)
+            as_blocks(z_side, fetched_unit(j), c)
 
     def on_y(kind, j):
         def act():
             y_arrival(kind, j).wait_recv()
             core_copy(kind, fetched + j).start()
-            as_blocks((x_side, z_side)[kind], plane_delay(j), c)
+            as_blocks((x_side, z_side)[kind], plane_unit(j), c)
 
         act() if kind == 0 else pl.when(has_z_from)(act)
 
-    for j in range(fetched + 4):
+    def on_core(kind, i):
+        def act():
+            core_arrival(kind, i).wait_recv()
+            as_blocks((x_side, z_side)[kind], core_unit(i), 1 - c)
+
+        act() if kind == 0 else pl.when(has_z_from)(act)
+
+    for j in range(fetched + 3):
         if j < fetched:
             on_x(j)
         if 0 <= j - 1 < fetched:
             on_z(j - 1)
-        if 0 <= j - 2 < ONLY:
-            on_y(0, j - 2)
-        if 0 <= j - 4 < ONLY:
-            on_y(1, j - 4)
+        if j >= 3 and j % 2 == 1 and (j - 3) // 2 < ONLY:
+            on_y(0, (j - 3) // 2)
+        if j >= 4 and j % 2 == 0 and (j - 4) // 2 < ONLY:
+            on_y(1, (j - 4) // 2)
+        if 0 <= j - 2 < fetched:
+            on_core(0, j - 2)
+        if 0 <= j - 3 < fetched:
+            on_core(1, j - 3)
         if j < tiles:
             first_coupling(j)
         if j < delays:
-            as_blocks(1, j, 0)
-            as_blocks(1, j, 1)
+            for i in range(PARTS * j, PARTS * (j + 1)):
+                as_blocks(1, i, 0)
+                as_blocks(1, i, 1)
+    for j in range(ONLY):
+        on_core(0, fetched + j)
+        on_core(1, fetched + j)
 
     load_ret.wait()
     for one in small:
         one.wait()
-    for i in range(delays):
-        core_arrival(0, i).wait_recv()
-        as_blocks(x_side, core_delay(i), 1 - c)
-
-    @pl.when(has_z_from)
-    def _():
-        for i in range(delays):
-            core_arrival(1, i).wait_recv()
-            as_blocks(z_side, core_delay(i), 1 - c)
-
     limit = live[0]
     none = jnp.zeros((waves, BLK), jnp.bfloat16)
 
@@ -331,7 +340,7 @@
         prods[step, BLK:, :] = low
         return 0
 
-    lax.fori_loop(0, slots // UNROLL, some_slots, 0, unroll=2)
+    lax.fori_loop(0, slots // UNROLL, some_slots, 0, unroll=4)
     total = jnp.zeros((2 * BLK, rb * waves), jnp.float32)
     for step in range(0, slots // UNROLL, 4):
         chosen = []
@@ -437,14 +446,14 @@
     for j in range(fetched):
         x_copy(j).wait_send()
         pl.when(has_z_to)(lambda: z_copy(j).wait_send())
-    for i in range(delays):
+    for i in range(units):
         core_copy(0, i).wait_send()
     for j in range(ONLY):
         y_copy(0, j).wait_send()
 
     @pl.when(has_z_from)
     def _():
-        for i in range(delays):
+        for i in range(units):
             core_copy(1, i).wait_send()
         for j in range(ONLY):
             y_copy(1, j).wait_send()
@@ -476,7 +485,8 @@
     own_cols = incident.shape[1]
     slots = ret_values.shape[0]
     rb = own_cols // BLK
-    fetched = delays - ONLY
+    units = delays * PARTS
+    fetched = units - ONLY
     tiles = own_cols // TILE
     window_blocks = patch_cols // BLK
     dma = pltpu.SemaphoreType.DMA
@@ -515,8 +525,8 @@
             dma((fetched,)),
             dma((2, ONLY)),
             dma((2, ONLY)),
-            dma((2, delays)),
-            dma((2, delays)),
+            dma((2, units)),
+            dma((2, units)),
             dma((2 * (SWEEPS - 1),)),
             dma((2 * (SWEEPS - 1),)),
             dma((3, tiles)),

time: 58.1 us -> 56.4 us (0.971)
  Pallas kernels: 53.4 us -> 51.6 us
    pallas_call x1, Pallas kernels: 53.4 us -> 51.6 us  [body(): pl.pallas_call(functools.partial(kernel, n_patch), out_shape=(jax.ShapeDt...]
where the time goes in v5:
time: 56.4 us; the launch traced here: 56.2 us
  Pallas kernels  51.6 us (91%)
  local copies, waits for them, and re-layouts  1.67 us (3%)
  other arithmetic  1.58 us (3%)
  between operations  1.3 us (2%)
    pallas_call x1, Pallas kernels, body(): pl.pallas_call(functools.partial(kernel, n_patch), out_shape=(jax.ShapeDt...  51.6 us
    reshape x1, local copies, waits for them, and re-layouts, body(): newest.transpose(1, 0, 2).reshape(waves, patch_cols)  1.67 us
    div x1, other arithmetic, body(): numerator / self_term[None, :]  1.58 us

profile of v5, /device:TPU:0, one launch (start us, length us, event | category | flops | bytes accessed | tf_op | source)
XLA Modules:
  0.0 56.2 jit_solution(5192000681860090527)
XLA Ops:
  1.3 0.0 copy-start
  1.3 51.6 %shard_map.104 = (f32[16,2048]{1,0:T(8,128)}, bf16[4,16,2048]{2,1,0:T(8,128)(2,1)}) custom-call(f32[16,2048]{1,0:T(8,128)} %incident_hbm.1, f32[1,2048]{1,0:T(1,128)} %bitcast.6, bf16[2048,2304]{1,0:T(8,128)(2,1)} %near_hbm.1, bf16[8,16,8192]{2,1,0:T(8,128)(2,1)} %hist_hbm.1, bf16[256,128,128]{2,1,0:T(8,128)(2,1)} %ret_hbm.1, s32[256]{0:T(256)} %row_hbm.1, ...), custom_call_target="tpu_custom_call" | custom-call | flops 603979776 | bytes 19922944 | tf_op jit(solution)/shard_map/pallas_call | solution.py:494
  52.9 0.0 copy-done
  53.0 1.6 %broadcast_divide_fusion = f32[16,2048]{1,0:T(8,128)} fusion(f32[16,2048]{1,0:T(8,128)} %get-tuple-element.4, f32[2048]{0:T(1024)S(1)} %copy-done), kind=kLoop, calls=%fused_computation | loop fusion | flops 32768 | bytes 270336 | tf_op jit(solution)/shard_map/div | solution.py:555
  54.5 1.7 %copy.12 = bf16[4,2,8,2048]{3,2,0,1:T(8,128)(2,1)} copy(bf16[4,2,8,2048]{3,2,1,0:T(8,128)(2,1)} %bitcast.5) | data formatting | bytes 524288 | tf_op jit(solution)/shard_map/reshape | solution.py:555
Async XLA Ops:
  1.3 51.7 %copy-start = (f32[2048]{0:T(1024)S(1)}, f32[2048]{0:T(1024)}, u32[]{:S(2)}) copy-start(f32[2048]{0:T(1024)} %param.10) | copy-start | bytes 24580
